TPU v7x, 32 devices: a whole 2x2x4 slice. The times are simulated.
32 devices in a mesh: groups: 2 (over x), node: 16 (over z, y, core).
Axes of the slice: x: 2, y: 2, z: 4, core: 2. Of those that a mesh axis runs over, the one named last changes fastest.
Arguments:
- child_query: bfloat16 [3072, 64, 576], P(('groups', 'node')), parts along dimension 0, may hold values from -24 to 24
- parent_cache: bfloat16 [32, 384, 576], P(('groups', 'node')), parts along dimension 0, may hold values from -4 to 4
- child_latent: bfloat16 [3072, 576], P(('groups', 'node')), parts along dimension 0, may hold values from -4 to 4
- parent_place: int32 [32], P('groups'), parts along dimension 0, may hold values from 0 to 15, each once
- child_parent: int32 [3072, 1], P(('groups', 'node')), parts along dimension 0, may hold values from 0 to 15; in each aligned block of 96 rows (0 to 95, 96 to 191, ...) at most 12 rows name the same one
- live_rows: int32 [32], P(('groups', 'node')), parts along dimension 0, may hold values from 72 to 96, as said below
Outputs:
- attended: bfloat16 [3072, 64, 512], P(('groups', 'node')), parts along dimension 0
There are 2 independent parts, one for each index of `groups`. A program takes and returns all parts, laid end to end along the dimension named above; each array names one. Nothing has to cross between parts.
Inputs may be any that keep to these rules, and one draw needn't show every extreme that they name: `child_parent`: within the rows of one device at most 12 rows name the same parent, and some device has exactly 12 rows naming one parent. `live_rows`: some device has all 96 slots live.
All inputs are finite; a program needn't handle non-finite values.
Results may differ from a plain program's by a relative error of at most 0.0047.
Values may be sent and summed in bfloat16 or wider, within the bound.
No kernel may reach another device: no remote copies, remote signals or barrier semaphores. Data moves between devices by JAX's collectives and lax.ppermute only.
A program may use at most 192 MiB of HBM per device.

v0:
```python
import math

import jax
import jax.numpy as jnp
from jax import lax
from jax.sharding import PartitionSpec as P

LAT = 512


SCALE = 0.07216878364870322


def softmax_parts(scores, own_score):
    highest = jnp.maximum(jnp.max(scores, axis=-1), own_score)
    expo = jnp.exp(scores - highest[..., None])
    own_expo = jnp.exp(own_score - highest)
    total = jnp.sum(expo, axis=-1) + own_expo
    return ((expo / total[..., None]).astype(jnp.bfloat16), (own_expo / total).astype(jnp.bfloat16))


def shards(child_query, parent_cache, child_latent, parent_place, child_parent, live_rows):
    row_total = child_query.shape[0]
    head_count = child_query.shape[1]
    entry_width = child_query.shape[2]
    parent_total = parent_place.shape[0]
    row_index = jnp.arange(row_total, dtype=jnp.int32)
    live = row_index < live_rows[0]
    matches = child_parent[:, 0][:, None] == jnp.arange(parent_total, dtype=jnp.int32)[None, :]
    stored_at = jnp.sum(jnp.where(matches, parent_place[None, :], 0), axis=1)
    everything = lax.all_gather(parent_cache, "node", axis=0, tiled=True)
    block_rows = math.gcd(row_total, 16)
    block_count = row_total // block_rows

    def one_block(inputs):
        query, latent, place = inputs
        cache = everything[place]
        scores = (
            jnp.einsum("bhk,bpk->bhp", query, cache, preferred_element_type=jnp.float32) * SCALE
        )
        own_score = (
            jnp.einsum("bhk,bk->bh", query, latent, preferred_element_type=jnp.float32) * SCALE
        )
        weights, own_weight = softmax_parts(scores, own_score)
        mixed = jnp.einsum(
            "bhp,bpv->bhv", weights, cache[:, :, :LAT], preferred_element_type=jnp.float32
        )
        mixed = mixed + own_weight.astype(jnp.float32)[..., None] * latent[:, None, :LAT].astype(
            jnp.float32
        )
        return mixed.astype(jnp.bfloat16)

    result = lax.map(
        one_block,
        (
            child_query.reshape(block_count, block_rows, head_count, entry_width),
            child_latent.reshape(block_count, block_rows, entry_width),
            stored_at.reshape(block_count, block_rows),
        ),
    )
    result = result.reshape(row_total, head_count, LAT)
    return jnp.where(live[:, None, None], result, jnp.zeros_like(result))


def solution(mesh):
    return jax.shard_map(
        shards,
        mesh=mesh,
        in_specs=(
            P(("groups", "node"), None, None),
            P(("groups", "node"), None, None),
            P(("groups", "node"), None),
            P("groups"),
            P(("groups", "node"), None),
            P(("groups", "node")),
        ),
        out_specs=P(("groups", "node"), None, None),
        check_vma=False,
    )
```

profile of v0, /device:TPU:0, one launch (start us, length us, event | category | flops | bytes accessed | tf_op | source)
XLA Modules:
  0.0 222.4 jit_solution(7488766757238307617)
XLA Ops:
  6.5 0.0 all-gather.2.cloned.1.call-start
  6.5 0.7 all-gather.2.cloned.1.call-update
  7.3 0.8 select_reduce_fusion
  8.0 0.1 reshape.51
  8.8 70.2 %all-gather.2.cloned.1.call-done = bf16[16,384,576]{1,2,0:T(8,128)(2,1)} async-done(((bf16[1,384,576]{1,2,0:T(8,128)(2,1)}), bf16[16,384,576]{1,2,0:T(8,128)(2,1)}) %all-gather.2.cloned.1.call-update) | async-done | bytes 7077904 | tf_op jit(solution)/shard_map/all_gather | solution.py:31
  79.0 10.1 %copy.12 = bf16[16,384,576]{2,1,0:T(8,128)(2,1)} copy(bf16[16,384,576]{1,2,0:T(8,128)(2,1)} %all-gather.2.cloned.1.call-done) | data formatting | bytes 14155776 | tf_op jit(solution)/shard_map/while | solution.py:53
  89.1 120.5 %while.10 = (s32[]{:T(128)}, bf16[6,16,64,512]{3,2,1,0:T(8,128)(2,1)}, bf16[6,16,64,576]{3,2,1,0:T(8,128)(2,1)}, s32[6,16]{1,0:T(8,128)S(1)}, bf16[16,384,576]{2...) while((s32[]{:T(128)}, bf16[6,16,64,512]{3,2,1,0:T(8,128)(2,1)}, ...), condition=%wide.region_4.5_spmd, body=%wide.region_1.4_spmd.sunk | while | flops 861159488 | bytes 65247088 | solution.py:53
  89.2 8.1 %gather_fusion = bf16[16,384,576]{2,1,0:T(8,128)(2,1)} fusion(bf16[16,384,576]{2,1,0:T(8,128)(2,1)} %get-tuple-element.135, s32[1024]{0:T(1024)S(1)} %pad_clamp_fusion.2), kind=kCustom, calls=%fused_computation.clone.1 | custom fusion | bytes 14155840 | tf_op jit(solution)/shard_map/while/body/eval_jaxpr/gather | solution.py:37
  97.2 0.0 copy-start
  97.2 6.5 %fusion.42 = (f32[16,64]{1,0:T(8,128)S(1)}, f32[16,64,384]{2,1,0:T(8,128)S(1)}) fusion(bf16[16,384,576]{2,1,0:T(8,128)(2,1)} %gather_fusion, bf16[6,16,64,576]{3,2,1,0:T(8,128)(2,1)} %get-tuple-element.133, s32[]{:T(128)} %get-tuple-element.124), kind=kOutput, calls=%fused_computation.37.clone.1 | convolution fusion | flops 453770240 | bytes 10752512 | tf_op jit(solution)/shard_map/while/body/eval_jaxpr/bhk,bpk->bhp/dot_general | solution.py:39
  103.7 0.7 dynamic-slice_bitcast_fusion.3
  104.4 1.8 fusion.43
  106.3 0.6 fusion.44
  106.9 0.0 copy-done
  106.9 2.3 %fusion.46 = bf16[6,16,64,512]{3,2,1,0:T(8,128)(2,1)} fusion(bf16[6,16,64,512]{3,2,1,0:T(8,128)(2,1)} %get-tuple-element.125, s32[]{:T(128)} %get-tuple-element.124, bf16[16,384,576]{2,1,0:T(8,128)(2,1)S(1)} %copy-done, f32[16,512]{1,0:T(8,128)S(1)} %slice_convert_fusion.2, f32[16,64]{1,0:T(8,128)S(1)} %get-tuple-element.115, ...), kind=kOutput, calls=%fused_computation.9.clone.1 | convolution fusion | flops 405405696 | bytes 8970752 | tf_op jit(solution)/shard_map/while/body/eval_jaxpr/bhp,bpv->bhv/dot_general | solution.py:45
  109.2 8.0 %gather_fusion = bf16[16,384,576]{2,1,0:T(8,128)(2,1)} fusion(bf16[16,384,576]{2,1,0:T(8,128)(2,1)} %get-tuple-element.135, s32[1024]{0:T(1024)S(1)} %pad_clamp_fusion.2), kind=kCustom, calls=%fused_computation.clone.1 | custom fusion | bytes 14155840 | tf_op jit(solution)/shard_map/while/body/eval_jaxpr/gather | solution.py:37
  117.3 0.0 copy-start
  117.3 6.5 %fusion.42 = (f32[16,64]{1,0:T(8,128)S(1)}, f32[16,64,384]{2,1,0:T(8,128)S(1)}) fusion(bf16[16,384,576]{2,1,0:T(8,128)(2,1)} %gather_fusion, bf16[6,16,64,576]{3,2,1,0:T(8,128)(2,1)} %get-tuple-element.133, s32[]{:T(128)} %get-tuple-element.124), kind=kOutput, calls=%fused_computation.37.clone.1 | convolution fusion | flops 453770240 | bytes 10752512 | tf_op jit(solution)/shard_map/while/body/eval_jaxpr/bhk,bpk->bhp/dot_general | solution.py:39
  123.7 0.7 dynamic-slice_bitcast_fusion.3
  124.5 1.8 fusion.43
  126.3 0.6 fusion.44
  126.9 0.0 copy-done
  126.9 2.3 %fusion.46 = bf16[6,16,64,512]{3,2,1,0:T(8,128)(2,1)} fusion(bf16[6,16,64,512]{3,2,1,0:T(8,128)(2,1)} %get-tuple-element.125, s32[]{:T(128)} %get-tuple-element.124, bf16[16,384,576]{2,1,0:T(8,128)(2,1)S(1)} %copy-done, f32[16,512]{1,0:T(8,128)S(1)} %slice_convert_fusion.2, f32[16,64]{1,0:T(8,128)S(1)} %get-tuple-element.115, ...), kind=kOutput, calls=%fused_computation.9.clone.1 | convolution fusion | flops 405405696 | bytes 8970752 | tf_op jit(solution)/shard_map/while/body/eval_jaxpr/bhp,bpv->bhv/dot_general | solution.py:45
  129.3 8.1 %gather_fusion = bf16[16,384,576]{2,1,0:T(8,128)(2,1)} fusion(bf16[16,384,576]{2,1,0:T(8,128)(2,1)} %get-tuple-element.135, s32[1024]{0:T(1024)S(1)} %pad_clamp_fusion.2), kind=kCustom, calls=%fused_computation.clone.1 | custom fusion | bytes 14155840 | tf_op jit(solution)/shard_map/while/body/eval_jaxpr/gather | solution.py:37
  137.3 0.0 copy-start
  137.4 6.5 %fusion.42 = (f32[16,64]{1,0:T(8,128)S(1)}, f32[16,64,384]{2,1,0:T(8,128)S(1)}) fusion(bf16[16,384,576]{2,1,0:T(8,128)(2,1)} %gather_fusion, bf16[6,16,64,576]{3,2,1,0:T(8,128)(2,1)} %get-tuple-element.133, s32[]{:T(128)} %get-tuple-element.124), kind=kOutput, calls=%fused_computation.37.clone.1 | convolution fusion | flops 453770240 | bytes 10752512 | tf_op jit(solution)/shard_map/while/body/eval_jaxpr/bhk,bpk->bhp/dot_general | solution.py:39
  143.8 0.7 dynamic-slice_bitcast_fusion.3
  144.6 1.8 fusion.43
  146.4 0.6 fusion.44
  147.0 0.0 copy-done
  147.0 2.3 %fusion.46 = bf16[6,16,64,512]{3,2,1,0:T(8,128)(2,1)} fusion(bf16[6,16,64,512]{3,2,1,0:T(8,128)(2,1)} %get-tuple-element.125, s32[]{:T(128)} %get-tuple-element.124, bf16[16,384,576]{2,1,0:T(8,128)(2,1)S(1)} %copy-done, f32[16,512]{1,0:T(8,128)S(1)} %slice_convert_fusion.2, f32[16,64]{1,0:T(8,128)S(1)} %get-tuple-element.115, ...), kind=kOutput, calls=%fused_computation.9.clone.1 | convolution fusion | flops 405405696 | bytes 8970752 | tf_op jit(solution)/shard_map/while/body/eval_jaxpr/bhp,bpv->bhv/dot_general | solution.py:45
  149.4 8.0 %gather_fusion = bf16[16,384,576]{2,1,0:T(8,128)(2,1)} fusion(bf16[16,384,576]{2,1,0:T(8,128)(2,1)} %get-tuple-element.135, s32[1024]{0:T(1024)S(1)} %pad_clamp_fusion.2), kind=kCustom, calls=%fused_computation.clone.1 | custom fusion | bytes 14155840 | tf_op jit(solution)/shard_map/while/body/eval_jaxpr/gather | solution.py:37
  157.4 0.0 copy-start
  157.4 6.5 %fusion.42 = (f32[16,64]{1,0:T(8,128)S(1)}, f32[16,64,384]{2,1,0:T(8,128)S(1)}) fusion(bf16[16,384,576]{2,1,0:T(8,128)(2,1)} %gather_fusion, bf16[6,16,64,576]{3,2,1,0:T(8,128)(2,1)} %get-tuple-element.133, s32[]{:T(128)} %get-tuple-element.124), kind=kOutput, calls=%fused_computation.37.clone.1 | convolution fusion | flops 453770240 | bytes 10752512 | tf_op jit(solution)/shard_map/while/body/eval_jaxpr/bhk,bpk->bhp/dot_general | solution.py:39
  163.9 0.7 dynamic-slice_bitcast_fusion.3
  164.6 1.8 fusion.43
  166.5 0.6 fusion.44
  167.1 0.0 copy-done
  167.1 2.3 %fusion.46 = bf16[6,16,64,512]{3,2,1,0:T(8,128)(2,1)} fusion(bf16[6,16,64,512]{3,2,1,0:T(8,128)(2,1)} %get-tuple-element.125, s32[]{:T(128)} %get-tuple-element.124, bf16[16,384,576]{2,1,0:T(8,128)(2,1)S(1)} %copy-done, f32[16,512]{1,0:T(8,128)S(1)} %slice_convert_fusion.2, f32[16,64]{1,0:T(8,128)S(1)} %get-tuple-element.115, ...), kind=kOutput, calls=%fused_computation.9.clone.1 | convolution fusion | flops 405405696 | bytes 8970752 | tf_op jit(solution)/shard_map/while/body/eval_jaxpr/bhp,bpv->bhv/dot_general | solution.py:45
  169.4 8.1 %gather_fusion = bf16[16,384,576]{2,1,0:T(8,128)(2,1)} fusion(bf16[16,384,576]{2,1,0:T(8,128)(2,1)} %get-tuple-element.135, s32[1024]{0:T(1024)S(1)} %pad_clamp_fusion.2), kind=kCustom, calls=%fused_computation.clone.1 | custom fusion | bytes 14155840 | tf_op jit(solution)/shard_map/while/body/eval_jaxpr/gather | solution.py:37
  177.5 0.0 copy-start
  177.5 6.5 %fusion.42 = (f32[16,64]{1,0:T(8,128)S(1)}, f32[16,64,384]{2,1,0:T(8,128)S(1)}) fusion(bf16[16,384,576]{2,1,0:T(8,128)(2,1)} %gather_fusion, bf16[6,16,64,576]{3,2,1,0:T(8,128)(2,1)} %get-tuple-element.133, s32[]{:T(128)} %get-tuple-element.124), kind=kOutput, calls=%fused_computation.37.clone.1 | convolution fusion | flops 453770240 | bytes 10752512 | tf_op jit(solution)/shard_map/while/body/eval_jaxpr/bhk,bpk->bhp/dot_general | solution.py:39
  184.0 0.7 dynamic-slice_bitcast_fusion.3
  184.7 1.8 fusion.43
  186.6 0.6 fusion.44
  187.2 0.0 copy-done
  187.2 2.3 %fusion.46 = bf16[6,16,64,512]{3,2,1,0:T(8,128)(2,1)} fusion(bf16[6,16,64,512]{3,2,1,0:T(8,128)(2,1)} %get-tuple-element.125, s32[]{:T(128)} %get-tuple-element.124, bf16[16,384,576]{2,1,0:T(8,128)(2,1)S(1)} %copy-done, f32[16,512]{1,0:T(8,128)S(1)} %slice_convert_fusion.2, f32[16,64]{1,0:T(8,128)S(1)} %get-tuple-element.115, ...), kind=kOutput, calls=%fused_computation.9.clone.1 | convolution fusion | flops 405405696 | bytes 8970752 | tf_op jit(solution)/shard_map/while/body/eval_jaxpr/bhp,bpv->bhv/dot_general | solution.py:45
  189.5 8.1 %gather_fusion = bf16[16,384,576]{2,1,0:T(8,128)(2,1)} fusion(bf16[16,384,576]{2,1,0:T(8,128)(2,1)} %get-tuple-element.135, s32[1024]{0:T(1024)S(1)} %pad_clamp_fusion.2), kind=kCustom, calls=%fused_computation.clone.1 | custom fusion | bytes 14155840 | tf_op jit(solution)/shard_map/while/body/eval_jaxpr/gather | solution.py:37
  197.6 0.0 copy-start
  197.6 6.5 %fusion.42 = (f32[16,64]{1,0:T(8,128)S(1)}, f32[16,64,384]{2,1,0:T(8,128)S(1)}) fusion(bf16[16,384,576]{2,1,0:T(8,128)(2,1)} %gather_fusion, bf16[6,16,64,576]{3,2,1,0:T(8,128)(2,1)} %get-tuple-element.133, s32[]{:T(128)} %get-tuple-element.124), kind=kOutput, calls=%fused_computation.37.clone.1 | convolution fusion | flops 453770240 | bytes 10752512 | tf_op jit(solution)/shard_map/while/body/eval_jaxpr/bhk,bpk->bhp/dot_general | solution.py:39
  204.1 0.7 dynamic-slice_bitcast_fusion.3
  204.8 1.8 fusion.43
  206.6 0.6 fusion.44
  207.3 0.0 copy-done
  207.3 2.3 %fusion.46 = bf16[6,16,64,512]{3,2,1,0:T(8,128)(2,1)} fusion(bf16[6,16,64,512]{3,2,1,0:T(8,128)(2,1)} %get-tuple-element.125, s32[]{:T(128)} %get-tuple-element.124, bf16[16,384,576]{2,1,0:T(8,128)(2,1)S(1)} %copy-done, f32[16,512]{1,0:T(8,128)S(1)} %slice_convert_fusion.2, f32[16,64]{1,0:T(8,128)S(1)} %get-tuple-element.115, ...), kind=kOutput, calls=%fused_computation.9.clone.1 | convolution fusion | flops 405405696 | bytes 8970752 | tf_op jit(solution)/shard_map/while/body/eval_jaxpr/bhp,bpv->bhv/dot_general | solution.py:45
  209.6 6.0 %bitcast_select_fusion = bf16[96,64,512]{2,1,0:T(8,128)(2,1)} fusion(bf16[6,16,64,512]{3,2,1,0:T(8,128)(2,1)} %get-tuple-element.37, pred[96]{0:T(512)(128)(4,1)S(1)} %iota_compare_fusion.1), kind=kLoop, calls=%fused_computation.33 | loop fusion | flops 3145728 | bytes 12583008 | tf_op jit(solution)/shard_map/jit(_where)/select_n | solution.py:62
  (32 shorter events, 0.3 us)
Async XLA Ops:
  6.5 72.5 %all-gather.2.cloned.1.call-start = ((), (), s32[]{:S(2)}) async-start(), calls=%async_computation | async-start | bytes 7520256 | tf_op jit(solution)/shard_map/all_gather | solution.py:31
  97.2 9.7 %copy-start = (bf16[16,384,576]{2,1,0:T(8,128)(2,1)S(1)}, bf16[16,384,576]{2,1,0:T(8,128)(2,1)}, u32[]{:S(2)}) copy-start(bf16[16,384,576]{2,1,0:T(8,128)(2,1)} %gather_fusion) | copy-start | bytes 21233668 | tf_op jit(solution)/shard_map/while
  117.3 9.7 %copy-start = (bf16[16,384,576]{2,1,0:T(8,128)(2,1)S(1)}, bf16[16,384,576]{2,1,0:T(8,128)(2,1)}, u32[]{:S(2)}) copy-start(bf16[16,384,576]{2,1,0:T(8,128)(2,1)} %gather_fusion) | copy-start | bytes 21233668 | tf_op jit(solution)/shard_map/while
  137.3 9.7 %copy-start = (bf16[16,384,576]{2,1,0:T(8,128)(2,1)S(1)}, bf16[16,384,576]{2,1,0:T(8,128)(2,1)}, u32[]{:S(2)}) copy-start(bf16[16,384,576]{2,1,0:T(8,128)(2,1)} %gather_fusion) | copy-start | bytes 21233668 | tf_op jit(solution)/shard_map/while
  157.4 9.7 %copy-start = (bf16[16,384,576]{2,1,0:T(8,128)(2,1)S(1)}, bf16[16,384,576]{2,1,0:T(8,128)(2,1)}, u32[]{:S(2)}) copy-start(bf16[16,384,576]{2,1,0:T(8,128)(2,1)} %gather_fusion) | copy-start | bytes 21233668 | tf_op jit(solution)/shard_map/while
  177.5 9.7 %copy-start = (bf16[16,384,576]{2,1,0:T(8,128)(2,1)S(1)}, bf16[16,384,576]{2,1,0:T(8,128)(2,1)}, u32[]{:S(2)}) copy-start(bf16[16,384,576]{2,1,0:T(8,128)(2,1)} %gather_fusion) | copy-start | bytes 21233668 | tf_op jit(solution)/shard_map/while
  197.6 9.7 %copy-start = (bf16[16,384,576]{2,1,0:T(8,128)(2,1)S(1)}, bf16[16,384,576]{2,1,0:T(8,128)(2,1)}, u32[]{:S(2)}) copy-start(bf16[16,384,576]{2,1,0:T(8,128)(2,1)} %gather_fusion) | copy-start | bytes 21233668 | tf_op jit(solution)/shard_map/while
Sparse Core Ops, SparseCore 0:
  9.6 69.3 all-gather.1
where the time goes:
time: 224 us; the launch traced here: 222 us
  waiting for transfers between devices  70.9 us (32%)
  matrix products  63.8 us (28%)
  local copies, waits for them, and re-layouts  62.9 us (28%)
  between operations  14.1 us (6%)
  other arithmetic  10.5 us (5%)
    all_gather x1, waiting for transfers between devices, shards(): everything = lax.all_gather(parent_cache, 'node', axis=0, tiled=True)  70.2 us
    gather x6, local copies, waits for them, and re-layouts, one_block(): cache = everything[place]  48.3 us
    dot_general x6, matrix products, one_block(): jnp.einsum('bhk,bpk->bhp', query, cache, preferred_element_type=jnp.float32)  38.9 us
    dot_general x6, matrix products, one_block(): jnp.einsum('bhp,bpv->bhv', weights, cache[:, :, :LAT], preferred_element_...  14 us
    dot_general x6, matrix products, one_block(): jnp.einsum('bhk,bk->bh', query, latent, preferred_element_type=jnp.float32)  10.9 us
    while x1, local copies, waits for them, and re-layouts, shards(): lax.map(one_block, (child_query.reshape(block_count, block_rows, head_cou...  10.1 us
    select_n x1, other arithmetic, shards(): return jnp.where(live[:, None, None], result, jnp.zeros_like(result))  5.97 us
  transfers between devices with their start and end apart: 1, of which 1 were waited for; matrix products, arithmetic and copies ran while one was open for 0% of the time, Pallas kernels for 0%

commit v1 on v0

v1 whole, which is shorter than its diff:
```python
import functools
import math

import jax
import jax.numpy as jnp
import numpy as np
from jax import lax
from jax.experimental import pallas as pl
from jax.experimental.pallas import tpu as pltpu
from jax.sharding import PartitionSpec as P

LAT = 512
SCALE = 0.07216878364870322
BLOCK = 4
ANY = pl.BlockSpec(memory_space=pl.ANY)
VMEM = pl.BlockSpec(memory_space=pltpu.VMEM)
SMEM = pl.BlockSpec(memory_space=pltpu.SMEM)


def sort_kernel(order, query, sorted_rows, sem):
    rows = query.shape[0]

    def fetch(j):
        return pltpu.make_async_copy(query.at[order[j]], sorted_rows.at[j], sem)

    @pl.loop(0, rows)
    def _(j):
        fetch(j).start()

    @pl.loop(0, rows)
    def _(j):
        fetch(j).wait()


def sort_rows(order, query):
    rows, heads, depth = query.shape
    return pl.pallas_call(
        sort_kernel,
        out_shape=pltpu.VMEM((rows + BLOCK, heads, depth), query.dtype),
        in_specs=[SMEM, ANY],
        out_specs=VMEM,
        scratch_shapes=[pltpu.SemaphoreType.DMA],
        compiler_params=pltpu.CompilerParams(vmem_limit_bytes=1024 * 1024),
        cost_estimate=pl.CostEstimate(flops=0, bytes_accessed=2 * query.size * 2, transcendentals=0),
    )(order, query)


def attend_kernel(first, arrays, aliased, order, starts, query, own, *refs):
    slots = refs[:arrays]
    refs = refs[arrays + (1 if aliased else 0):]
    out, kv, even, odd, ov, zeros, blocks, kv_sem, out_sem = refs
    count = arrays
    prefix = slots[0].shape[-1]
    width = kv.shape[2]
    rows = order.shape[0]
    heads = query.shape[1]
    size = BLOCK * heads
    dead = starts[starts.shape[0] - 1]
    base = starts[first]
    end = starts[first + count]

    def fetch_slot(s):
        return (
            pltpu.make_async_copy(slots[s], kv.at[s, :, pl.ds(0, prefix)], kv_sem.at[s, 0]),
            pltpu.make_async_copy(own, kv.at[s, :, pl.ds(prefix, width - prefix)], kv_sem.at[s, 1]),
        )

    for s in range(count):

        @pl.when(starts[first + s + 1] > starts[first + s])
        def _():
            for copy in fetch_slot(s):
                copy.start()

    if not aliased:
        zeros[...] = jnp.zeros_like(zeros)

        @pl.loop(dead, rows)
        def _(j):
            pltpu.make_async_copy(zeros, out.at[order[j]], out_sem).start()

    number = jnp.int32(0)
    for s in range(count):
        lo, hi = starts[first + s], starts[first + s + 1]
        more = (hi - lo + BLOCK - 1) // BLOCK

        def note(b, _):
            blocks[0, number + b] = s
            blocks[1, number + b] = lo + b * BLOCK
            blocks[2, number + b] = jnp.minimum(lo + (b + 1) * BLOCK, hi)
            return 0

        lax.fori_loop(0, more, note, 0)
        number = number + more
    for b in range(2):
        blocks[0, number + b] = 0
        blocks[1, number + b] = rows
        blocks[2, number + b] = rows

    for s in range(count):

        @pl.when(starts[first + s + 1] > starts[first + s])
        def _():
            for copy in fetch_slot(s):
                copy.wait()

    column = lax.broadcasted_iota(jnp.int32, (size, width), 1)
    row = lax.broadcasted_iota(jnp.int32, (size, width), 0) // heads
    offset = jnp.where(column < prefix, 0, column - prefix - row)

    def score(b, to):
        q = query[pl.ds(blocks[1, b], BLOCK)].reshape(size, query.shape[2])
        to[...] = jnp.dot(q, kv[blocks[0, b]], preferred_element_type=jnp.float32)

    def finish(b, scores):
        begin = blocks[1, b]
        seen = (column < prefix) | (offset == begin)
        s = jnp.where(seen, scores[...], -jnp.inf)
        top = jnp.max(s, axis=1, keepdims=True)
        expo = jnp.exp2((s - top) * (SCALE * math.log2(math.e)))
        total = jnp.sum(expo, axis=1, keepdims=True)
        weights = (expo * (1.0 / total)).astype(jnp.bfloat16)
        mixed = lax.dot_general(
            weights, kv[blocks[0, b], 0:LAT, :], (((1,), (1,)), ((), ())), preferred_element_type=jnp.float32
        )
        ov[pl.ds(begin, BLOCK)] = mixed.astype(jnp.bfloat16).reshape(BLOCK, heads, LAT)

    def send(b):
        @pl.loop(blocks[1, b], blocks[2, b])
        def _(j):
            pltpu.make_async_copy(ov.at[j], out.at[order[j]], out_sem).start()

    @pl.when(number > 0)
    def _():
        score(0, even)

        @pl.loop(0, (number + 1) // 2)
        def _(pair):
            b = pair * 2
            score(b + 1, odd)
            finish(b, even)
            score(b + 2, even)
            finish(b + 1, odd)
            send(b)
            send(b + 1)

    @pl.loop(base, end)
    def _(j):
        pltpu.make_async_copy(ov.at[j], out.at[order[j]], out_sem).wait()

    if not aliased:

        @pl.loop(dead, rows)
        def _(j):
            pltpu.make_async_copy(zeros, out.at[order[j]], out_sem).wait()


def attend(order, starts, first, query, own, slots, out=None):
    rows = order.shape[0]
    _, heads, depth = query.shape
    count = len(slots)
    prefix = slots[0].shape[-1]
    width = prefix + own.shape[1]
    aliased = out is not None
    operands = [order, starts, query, own, *slots] + ([out] if aliased else [])
    work = rows * heads * count // (starts.shape[0] - 1)
    return pl.pallas_call(
        functools.partial(attend_kernel, first, count, aliased),
        out_shape=jax.ShapeDtypeStruct((rows, heads, LAT), jnp.bfloat16),
        in_specs=[SMEM, SMEM, VMEM] + [ANY] * (len(operands) - 3),
        out_specs=ANY,
        scratch_shapes=[
            pltpu.VMEM((count, depth, width), jnp.bfloat16),
            pltpu.VMEM((BLOCK * heads, width), jnp.float32),
            pltpu.VMEM((BLOCK * heads, width), jnp.float32),
            pltpu.VMEM((rows + BLOCK, heads, LAT), jnp.bfloat16),
            pltpu.VMEM((heads, LAT), jnp.bfloat16),
            pltpu.SMEM((3, rows // BLOCK + count + 4), jnp.int32),
            pltpu.SemaphoreType.DMA((count, 2)),
            pltpu.SemaphoreType.DMA,
        ],
        input_output_aliases={len(operands) - 1: 0} if aliased else {},
        compiler_params=pltpu.CompilerParams(vmem_limit_bytes=20 * 1024 * 1024),
        cost_estimate=pl.CostEstimate(
            flops=2 * work * width * (depth + LAT),
            bytes_accessed=count * depth * width * 2 + work * LAT * 2,
            transcendentals=work * width,
        ),
    )(*operands)


def ring_of(nodes):
    chips = nodes // 2
    if chips == 8:
        return [0, 2, 4, 6, 7, 5, 3, 1]
    return list(range(chips))


def table(child_parent, parent_place, live_rows, ring, slot_of_distance, slot_count):
    rows = child_parent.shape[0]
    parents = parent_place.shape[0]
    chips = len(ring)
    me = lax.axis_index("node")
    core = me % 2
    position = np.zeros((parents,), np.int32)
    for at, chip in enumerate(ring):
        position[2 * chip] = position[2 * chip + 1] = at
    position = jnp.asarray(position)
    here = jnp.sum(jnp.where(jnp.arange(parents) == me, position, 0))
    ahead = jnp.where(core == 0, position - here, here - position)
    ahead = jnp.where(ahead < 0, ahead + chips, ahead)
    kind = 2 * ahead + jnp.where(jnp.arange(parents) % 2 == core, 0, 1)
    numbers = jnp.asarray(np.asarray(slot_of_distance, np.int32).reshape(-1))
    kinds = jnp.arange(parents, dtype=jnp.int32)
    slot_of_place = jnp.sum(jnp.where(kind[:, None] == kinds[None, :], numbers[None, :], 0), axis=1)
    slot_of_parent = jnp.sum(
        jnp.where(parent_place[:, None] == kinds[None, :], slot_of_place[None, :], 0), axis=1
    )
    named = child_parent == kinds[None, :]
    index = jnp.arange(rows, dtype=jnp.int32)
    slot = jnp.sum(jnp.where(named, slot_of_parent[None, :], 0), axis=1)
    slot = jnp.where(index < live_rows[0], slot, slot_count)
    key = slot * rows + index
    place = jnp.sum((key[None, :] < key[:, None]).astype(jnp.int32), axis=1)
    order = jnp.sum(jnp.where(place[:, None] == index[None, :], index[:, None], 0), axis=0)
    starts = jnp.sum(
        (slot[:, None] < jnp.arange(slot_count + 1, dtype=jnp.int32)[None, :]).astype(jnp.int32), axis=0
    )
    return order, starts, place


def shards(nodes, child_query, parent_cache, child_latent, parent_place, child_parent, live_rows):
    rows = child_query.shape[0]
    ring = ring_of(nodes)
    chips = len(ring)
    along = [(2 * ring[i], 2 * ring[(i + 1) % chips]) for i in range(chips)]
    along += [(2 * ring[(i + 1) % chips] + 1, 2 * ring[i] + 1) for i in range(chips)]
    across = [(i, i ^ 1) for i in range(nodes)]

    mine = jnp.swapaxes(parent_cache[0], 0, 1)
    other = lax.ppermute(mine, "node", across)
    phases = [[mine, other]]
    slot_of_distance = [[0, 1]] + [[0, 0] for _ in range(chips - 1)]
    number = 2
    streams = [mine, other]
    for k in range(1, chips // 2 + 1):
        both = 2 * k < chips
        streams = [lax.ppermute(a, "node", along) for a in streams[: 2 if both else 1]]
        for which, a in enumerate(streams):
            phases.append([a, lax.ppermute(a, "node", across)])
            if both:
                slot_of_distance[chips - k][which] = number
                slot_of_distance[k][1 - which] = number + 1
            else:
                slot_of_distance[k] = [number, number + 1]
            number += 2

    order, starts, place = table(child_parent, parent_place, live_rows, ring, slot_of_distance, number)
    padded = -(-rows // 128) * 128
    pick = (place[:, None] == jnp.arange(padded, dtype=jnp.int32)[None, :]).astype(jnp.bfloat16)
    own = lax.dot_general(
        child_latent, pick, (((0,), (0,)), ((), ())), preferred_element_type=jnp.float32
    ).astype(jnp.bfloat16)
    query = sort_rows(order, child_query)
    out, first = None, 0
    for slots in phases:
        out = attend(order, starts, first, query, own, slots, out)
        first += len(slots)
    return out


def solution(mesh):
    return jax.shard_map(
        functools.partial(shards, mesh.shape["node"]),
        mesh=mesh,
        in_specs=(
            P(("groups", "node"), None, None),
            P(("groups", "node"), None, None),
            P(("groups", "node"), None),
            P("groups"),
            P(("groups", "node"), None),
            P(("groups", "node")),
        ),
        out_specs=P(("groups", "node"), None, None),
        check_vma=False,
    )
```

time: 224 us -> 78.3 us (0.35)
  the two profiles are of different devices: /device:TPU:0 before, /device:TPU:1 now
where the time goes in v1:
time: 78.3 us; the launch traced here: 78.5 us
  Pallas kernels  42.6 us (54%)
  starting transfers between devices  15.1 us (19%)
  waiting for transfers between devices  11 us (14%)
  other arithmetic  5.42 us (7%)
  local copies, waits for them, and re-layouts  3.24 us (4%)
  between operations  0.81 us (1%)
    pallas_call x8, Pallas kernels, attend(): pl.pallas_call(functools.partial(attend_kernel, first, count, aliased), o...  30.5 us
    pallas_call x1, Pallas kernels, sort_rows(): pl.pallas_call(sort_kernel, out_shape=pltpu.VMEM((rows + BLOCK, heads, de...  12.1 us
    ppermute x7, waiting for transfers between devices, shards(): lax.ppermute(a, 'node', along)  11 us
    ppermute x7, starting transfers between devices, shards(): lax.ppermute(a, 'node', along)  11 us
    ppermute x7, starting transfers between devices, shards(): phases.append([a, lax.ppermute(a, 'node', across)])  4.06 us
    unnamed x6, local copies, waits for them, and re-layouts  3.24 us
  transfers between devices with their start and end apart: 15, of which 5 were waited for; matrix products, arithmetic and copies ran while one was open for 7% of the time, Pallas kernels for 50%

profile of v1, /device:TPU:1, one launch (start us, length us, event | category | flops | bytes accessed | tf_op | source)
XLA Modules:
  0.0 78.5 jit_solution(10578545325882946779)
XLA Ops:
  0.0 0.0 copy-start
  0.0 0.1 collective-permute-start.5
  0.1 2.7 %collective-permute-start = (bf16[576,384]{1,0:T(8,128)(2,1)}, bf16[576,384]{1,0:T(8,128)(2,1)S(1)}, u32[]{:S(2)}, u32[]{:S(2)}) collective-permute-start(bf16[576,384]{1,0:T(8,128)(2,1)} %bitcast.10), channel_id=1, source_target_pairs={{0,4},{4,8},{8,12},{12,14},{14,10},{10,6},{6,2},{2,0},{5,1},{9,5},... | collective-permute-start | bytes 1327112 | tf_op jit(solution)/shard_map/ppermute | solution.py:248
  3.4 1.3 %fusion.2 = s32[]{:T(128)} fusion(s32[16]{0:T(128)} %constant.40.clone, s32[]{:T(128)S(6)} %axis_index.12), kind=kLoop, calls=%fused_computation.21 | loop fusion | flops 47 | bytes 72 | tf_op jit(solution)/shard_map/reduce_sum | solution.py:209
  4.7 0.0 collective-permute-done.5.refs_1_
  4.7 1.3 %collective-permute-start.6 = (bf16[576,384]{1,0:T(8,128)(2,1)S(1)}, bf16[576,384]{1,0:T(8,128)(2,1)S(1)}, u32[]{:S(2)}, u32[]{:S(2)}) collective-permute-start(bf16[576,384]{1,0:T(8,128)(2,1)S(1)} %collective-permute-done.5.refs_1_), channel_id=1, source_target_pairs={{0,4},{4,8},{8,12},{12,14},{14,10},{10,6},{6,2},{2,0},{5,1},{9,5},... | collective-permute-start | bytes 1327112 | tf_op jit(solution)/shard_map/ppermute | solution.py:248
  6.0 3.0 %collective-permute-done.refs_0_ = bf16[576,384]{1,0:T(8,128)(2,1)S(1)} collective-permute-done((bf16[576,384]{1,0:T(8,128)(2,1)}, bf16[576,384]{1,0:T(8,128)(2,1)S(1)}, u32[]{:S(2)}, u32[]{:S(2)}) %collective-permute-start) | collective-permute-done | bytes 442400 | tf_op jit(solution)/shard_map/ppermute | solution.py:248
  9.0 1.4 %collective-permute-start.1 = (bf16[576,384]{1,0:T(8,128)(2,1)S(1)}, bf16[576,384]{1,0:T(8,128)(2,1)S(1)}, u32[]{:S(2)}, u32[]{:S(2)}) collective-permute-start(bf16[576,384]{1,0:T(8,128)(2,1)S(1)} %collective-permute-done.refs_0_), channel_id=1, source_target_pairs={{0,4},{4,8},{8,12},{12,14},{14,10},{10,6},{6,2},{2,0},{5,1},{9,5},... | collective-permute-start | bytes 1327112 | tf_op jit(solution)/shard_map/ppermute | solution.py:248
  10.4 1.3 %fusion.3 = s32[16]{0:T(128)S(1)} fusion(s32[16]{0:T(128)} %constant.44, s32[16]{0:T(128)} %constant.40.clone, pred[]{:T(512)S(6)} %eq.93, s32[]{:T(128)S(6)} %select_n.63, s32[]{:T(128)} %fusion.2), kind=kLoop, calls=%fused_computation.22 | loop fusion | flops 256 | bytes 201 | tf_op jit(solution)/shard_map/add | solution.py:212
  11.7 0.8 %select_reduce_fusion.3 = s32[16]{0:T(128)S(1)} fusion(s32[16]{0:T(128)} %constant.41.clone, s32[16]{0:T(128)S(1)} %fusion.3), kind=kLoop, calls=%fused_computation.11 | loop fusion | flops 752 | bytes 192 | tf_op jit(solution)/shard_map/reduce_sum | solution.py:215
  12.6 0.8 %select_reduce_fusion.2 = s32[16]{0:T(128)S(1)} fusion(s32[16]{0:T(128)S(1)} %select_reduce_fusion.3, s32[16]{0:T(128)} %param.11), kind=kLoop, calls=%fused_computation.10 | loop fusion | flops 752 | bytes 192 | tf_op jit(solution)/shard_map/reduce_sum | solution.py:216
  13.4 0.3 collective-permute-done.6.refs_0_
  13.7 1.4 %collective-permute-start.7 = (bf16[576,384]{1,0:T(8,128)(2,1)S(1)}, bf16[576,384]{1,0:T(8,128)(2,1)S(1)}, u32[]{:S(2)}, u32[]{:S(2)}) collective-permute-start(bf16[576,384]{1,0:T(8,128)(2,1)S(1)} %collective-permute-done.6.refs_0_), channel_id=1, source_target_pairs={{0,4},{4,8},{8,12},{12,14},{14,10},{10,6},{6,2},{2,0},{5,1},{9,5},... | collective-permute-start | bytes 1327112 | tf_op jit(solution)/shard_map/ppermute | solution.py:248
  15.1 3.3 %collective-permute-done.1.refs_0_ = bf16[576,384]{1,0:T(8,128)(2,1)S(1)} collective-permute-done((bf16[576,384]{1,0:T(8,128)(2,1)S(1)}, bf16[576,384]{1,0:T(8,128)(2,1)S(1)}, u32[]{:S(2)}, u32[]{:S(2)}) %collective-permute-start.1) | collective-permute-done | bytes 442400 | tf_op jit(solution)/shard_map/ppermute | solution.py:248
  18.5 1.4 %collective-permute-start.2 = (bf16[576,384]{1,0:T(8,128)(2,1)S(1)}, bf16[576,384]{1,0:T(8,128)(2,1)S(1)}, u32[]{:S(2)}, u32[]{:S(2)}) collective-permute-start(bf16[576,384]{1,0:T(8,128)(2,1)S(1)} %collective-permute-done.1.refs_0_), channel_id=1, source_target_pairs={{0,4},{4,8},{8,12},{12,14},{14,10},{10,6},{6,2},{2,0},{5,1},{9,5},... | collective-permute-start | bytes 1327112 | tf_op jit(solution)/shard_map/ppermute | solution.py:248
  19.9 0.7 select_reduce_fusion.1
  20.6 1.3 %collective-permute-start.14 = (bf16[576,384]{1,0:T(8,128)(2,1)S(1)}, bf16[576,384]{1,0:T(8,128)(2,1)S(1)}, u32[]{:S(2)}, u32[]{:S(2)}) collective-permute-start(bf16[576,384]{1,0:T(8,128)(2,1)S(1)} %collective-permute-done.refs_0_), channel_id=1, source_target_pairs={{0,1},{1,0},{2,3},{3,2},{4,5},{5,4},{6,7},{7,6},{8,9},{9,8},{10,11... | collective-permute-start | bytes 1327112 | tf_op jit(solution)/shard_map/ppermute | solution.py:250
  21.9 0.1 collective-permute-start.13
  22.0 0.2 convert_reduce_fusion
  22.2 1.0 %collective-permute-done.7.refs_0_ = bf16[576,384]{1,0:T(8,128)(2,1)S(1)} collective-permute-done((bf16[576,384]{1,0:T(8,128)(2,1)S(1)}, bf16[576,384]{1,0:T(8,128)(2,1)S(1)}, u32[]{:S(2)}, u32[]{:S(2)}) %collective-permute-start.7) | collective-permute-done | bytes 442400 | tf_op jit(solution)/shard_map/ppermute | solution.py:248
  23.2 1.4 %collective-permute-start.8 = (bf16[576,384]{1,0:T(8,128)(2,1)S(1)}, bf16[576,384]{1,0:T(8,128)(2,1)S(1)}, u32[]{:S(2)}, u32[]{:S(2)}) collective-permute-start(bf16[576,384]{1,0:T(8,128)(2,1)S(1)} %collective-permute-done.7.refs_0_), channel_id=1, source_target_pairs={{0,4},{4,8},{8,12},{12,14},{14,10},{10,6},{6,2},{2,0},{5,1},{9,5},... | collective-permute-start | bytes 1327112 | tf_op jit(solution)/shard_map/ppermute | solution.py:248
  24.6 3.3 %collective-permute-done.2.refs_0_ = bf16[576,384]{1,0:T(8,128)(2,1)S(1)} collective-permute-done((bf16[576,384]{1,0:T(8,128)(2,1)S(1)}, bf16[576,384]{1,0:T(8,128)(2,1)S(1)}, u32[]{:S(2)}, u32[]{:S(2)}) %collective-permute-start.2) | collective-permute-done | bytes 442400 | tf_op jit(solution)/shard_map/ppermute | solution.py:248
  28.0 1.4 %collective-permute-start.3 = (bf16[576,384]{1,0:T(8,128)(2,1)S(1)}, bf16[576,384]{1,0:T(8,128)(2,1)S(1)}, u32[]{:S(2)}, u32[]{:S(2)}) collective-permute-start(bf16[576,384]{1,0:T(8,128)(2,1)S(1)} %collective-permute-done.2.refs_0_), channel_id=1, source_target_pairs={{0,4},{4,8},{8,12},{12,14},{14,10},{10,6},{6,2},{2,0},{5,1},{9,5},... | collective-permute-start | bytes 1327112 | tf_op jit(solution)/shard_map/ppermute | solution.py:248
  29.4 0.0 copy-done
  29.4 0.3 fusion.own
  29.6 1.3 %collective-permute-start.12 = (bf16[576,384]{1,0:T(8,128)(2,1)S(1)}, bf16[576,384]{1,0:T(8,128)(2,1)S(1)}, u32[]{:S(2)}, u32[]{:S(2)}) collective-permute-start(bf16[576,384]{1,0:T(8,128)(2,1)S(1)} %collective-permute-done.1.refs_0_), channel_id=1, source_target_pairs={{0,1},{1,0},{2,3},{3,2},{4,5},{5,4},{6,7},{7,6},{8,9},{9,8},{10,11... | collective-permute-start | bytes 1327112 | tf_op jit(solution)/shard_map/ppermute | solution.py:250
  31.0 0.0 collective-permute-done.14.refs_1_
  31.0 0.1 collective-permute-start.11
  31.0 0.1 select_reduce_fusion.order
  31.1 0.0 collective-permute-done.13.refs_1_
  31.1 0.5 collective-permute-start.10
  31.6 0.1 convert_reduce_fusion.1.starts
  31.7 0.0 copy-start.1
  31.8 3.2 %copy-done.1 = bf16[96,64,576]{2,1,0:T(8,128)(2,1)S(1)} copy-done((bf16[96,64,576]{2,1,0:T(8,128)(2,1)S(1)}, bf16[96,64,576]{2,1,0:T(8,128)(2,1)}, u32[]{:S(2)}) %copy-start.1) | copy-done | bytes 7077912
  35.0 0.0 copy-start.2
  35.0 12.1 %shard_map.82.query = bf16[100,64,576]{2,1,0:T(8,128)(2,1)S(1)} custom-call(s32[96]{0:T(128)S(1)} %select_reduce_fusion.order, bf16[96,64,576]{2,1,0:T(8,128)(2,1)S(1)} %copy-done.1), custom_call_target="tpu_custom_call" | custom-call | bytes 14155776 | tf_op jit(solution)/shard_map/pallas_call | solution.py:37
  47.1 0.0 collective-permute-done.8.refs_0_
  47.1 0.2 collective-permute-start.9
  47.3 0.0 copy-done.2
  47.3 3.7 %shard_map.83.refs_2_ = bf16[96,64,512]{2,1,0:T(8,128)(2,1)} custom-call(s32[96]{0:T(128)S(1)} %select_reduce_fusion.order, s32[17]{0:T(128)S(1)} %convert_reduce_fusion.1.starts, bf16[100,64,576]{2,1,0:T(8,128)(2,1)S(1)} %shard_map.82.query, bf16[576,128]{1,0:T(8,128)(2,1)S(1)} %fusion.own, bf16[576,384]{1,0:T(8,128)(2,1)S(1)} %bitcast.11, ...), custom_call_target="tpu_custom_call" | custom-call | flops 855638016 | bytes 1966080 | tf_op jit(solution)/shard_map/pallas_call | solution.py:167
  51.0 0.0 collective-permute-done.3.refs_0_
  51.0 0.6 collective-permute-start.4
  51.6 3.7 %shard_map.84.refs_2_ = bf16[96,64,512]{2,1,0:T(8,128)(2,1)} custom-call(s32[96]{0:T(128)S(1)} %select_reduce_fusion.order, s32[17]{0:T(128)S(1)} %convert_reduce_fusion.1.starts, bf16[100,64,576]{2,1,0:T(8,128)(2,1)S(1)} %shard_map.82.query, bf16[576,128]{1,0:T(8,128)(2,1)S(1)} %fusion.own, ...), custom_call_target="tpu_custom_call", output_to_operand_aliasing={{}: (6, {})} | custom-call | flops 855638016 | bytes 1966080 | tf_op jit(solution)/shard_map/pallas_call | solution.py:167
  55.4 3.7 %shard_map.85.refs_2_ = bf16[96,64,512]{2,1,0:T(8,128)(2,1)} custom-call(s32[96]{0:T(128)S(1)} %select_reduce_fusion.order, s32[17]{0:T(128)S(1)} %convert_reduce_fusion.1.starts, bf16[100,64,576]{2,1,0:T(8,128)(2,1)S(1)} %shard_map.82.query, bf16[576,128]{1,0:T(8,128)(2,1)S(1)} %fusion.own, ...), custom_call_target="tpu_custom_call", output_to_operand_aliasing={{}: (6, {})} | custom-call | flops 855638016 | bytes 1966080 | tf_op jit(solution)/shard_map/pallas_call | solution.py:167
  59.1 0.0 collective-permute-done.12.refs_1_
  59.1 3.8 %shard_map.86.refs_2_ = bf16[96,64,512]{2,1,0:T(8,128)(2,1)} custom-call(s32[96]{0:T(128)S(1)} %select_reduce_fusion.order, s32[17]{0:T(128)S(1)} %convert_reduce_fusion.1.starts, bf16[100,64,576]{2,1,0:T(8,128)(2,1)S(1)} %shard_map.82.query, bf16[576,128]{1,0:T(8,128)(2,1)S(1)} %fusion.own, ...), custom_call_target="tpu_custom_call", output_to_operand_aliasing={{}: (6, {})} | custom-call | flops 855638016 | bytes 1966080 | tf_op jit(solution)/shard_map/pallas_call | solution.py:167
  62.9 0.0 collective-permute-done.11.refs_1_
  62.9 3.7 %shard_map.87.refs_2_ = bf16[96,64,512]{2,1,0:T(8,128)(2,1)} custom-call(s32[96]{0:T(128)S(1)} %select_reduce_fusion.order, s32[17]{0:T(128)S(1)} %convert_reduce_fusion.1.starts, bf16[100,64,576]{2,1,0:T(8,128)(2,1)S(1)} %shard_map.82.query, bf16[576,128]{1,0:T(8,128)(2,1)S(1)} %fusion.own, ...), custom_call_target="tpu_custom_call", output_to_operand_aliasing={{}: (6, {})} | custom-call | flops 855638016 | bytes 1966080 | tf_op jit(solution)/shard_map/pallas_call | solution.py:167
  66.5 0.0 collective-permute-done.10.refs_1_
  66.6 4.6 %shard_map.88.refs_2_ = bf16[96,64,512]{2,1,0:T(8,128)(2,1)} custom-call(s32[96]{0:T(128)S(1)} %select_reduce_fusion.order, s32[17]{0:T(128)S(1)} %convert_reduce_fusion.1.starts, bf16[100,64,576]{2,1,0:T(8,128)(2,1)S(1)} %shard_map.82.query, bf16[576,128]{1,0:T(8,128)(2,1)S(1)} %fusion.own, ...), custom_call_target="tpu_custom_call", output_to_operand_aliasing={{}: (6, {})} | custom-call | flops 855638016 | bytes 1966080 | tf_op jit(solution)/shard_map/pallas_call | solution.py:167
  71.1 0.0 collective-permute-done.9.refs_1_
  71.1 3.7 %shard_map.89.refs_2_ = bf16[96,64,512]{2,1,0:T(8,128)(2,1)} custom-call(s32[96]{0:T(128)S(1)} %select_reduce_fusion.order, s32[17]{0:T(128)S(1)} %convert_reduce_fusion.1.starts, bf16[100,64,576]{2,1,0:T(8,128)(2,1)S(1)} %shard_map.82.query, bf16[576,128]{1,0:T(8,128)(2,1)S(1)} %fusion.own, ...), custom_call_target="tpu_custom_call", output_to_operand_aliasing={{}: (6, {})} | custom-call | flops 855638016 | bytes 1966080 | tf_op jit(solution)/shard_map/pallas_call | solution.py:167
  74.9 0.0 collective-permute-done.4.refs_1_
  74.9 3.6 %shard_map.90 = bf16[96,64,512]{2,1,0:T(8,128)(2,1)} custom-call(s32[96]{0:T(128)S(1)} %select_reduce_fusion.order, s32[17]{0:T(128)S(1)} %convert_reduce_fusion.1.starts, bf16[100,64,576]{2,1,0:T(8,128)(2,1)S(1)} %shard_map.82.query, bf16[576,128]{1,0:T(8,128)(2,1)S(1)} %fusion.own, ...), custom_call_target="tpu_custom_call", output_to_operand_aliasing={{}: (6, {})} | custom-call | flops 855638016 | bytes 1966080 | tf_op jit(solution)/shard_map/pallas_call | solution.py:167
  (1 shorter events, 0.0 us)
Async XLA Ops:
  0.0 29.4 %copy-start = (bf16[96,576]{1,0:T(8,128)(2,1)S(1)}, bf16[96,576]{1,0:T(8,128)(2,1)}, u32[]{:S(2)}) copy-start(bf16[96,576]{1,0:T(8,128)(2,1)} %param.10) | copy-start | bytes 331780
  0.0 4.7 %collective-permute-start.5 = (bf16[576,384]{1,0:T(8,128)(2,1)}, bf16[576,384]{1,0:T(8,128)(2,1)S(1)}, u32[]{:S(2)}, u32[]{:S(2)}) collective-permute-start(bf16[576,384]{1,0:T(8,128)(2,1)} %bitcast.9), channel_id=1, source_target_pairs={{0,1},{1,0},{2,3},{3,2},{4,5},{5,4},{6,7},{7,6},{8,9},{9,8},{10,11... | collective-permute-start | bytes 1327112 | tf_op jit(solution)/shard_map/ppermute | solution.py:241
  0.1 8.9 %collective-permute-start = (bf16[576,384]{1,0:T(8,128)(2,1)}, bf16[576,384]{1,0:T(8,128)(2,1)S(1)}, u32[]{:S(2)}, u32[]{:S(2)}) collective-permute-start(bf16[576,384]{1,0:T(8,128)(2,1)} %bitcast.10), channel_id=1, source_target_pairs={{0,4},{4,8},{8,12},{12,14},{14,10},{10,6},{6,2},{2,0},{5,1},{9,5},... | collective-permute-start | bytes 1327112 | tf_op jit(solution)/shard_map/ppermute | solution.py:248
  4.7 9.0 %collective-permute-start.6 = (bf16[576,384]{1,0:T(8,128)(2,1)S(1)}, bf16[576,384]{1,0:T(8,128)(2,1)S(1)}, u32[]{:S(2)}, u32[]{:S(2)}) collective-permute-start(bf16[576,384]{1,0:T(8,128)(2,1)S(1)} %collective-permute-done.5.refs_1_), channel_id=1, source_target_pairs={{0,4},{4,8},{8,12},{12,14},{14,10},{10,6},{6,2},{2,0},{5,1},{9,5},... | collective-permute-start | bytes 1327112 | tf_op jit(solution)/shard_map/ppermute | solution.py:248
  9.0 9.5 %collective-permute-start.1 = (bf16[576,384]{1,0:T(8,128)(2,1)S(1)}, bf16[576,384]{1,0:T(8,128)(2,1)S(1)}, u32[]{:S(2)}, u32[]{:S(2)}) collective-permute-start(bf16[576,384]{1,0:T(8,128)(2,1)S(1)} %collective-permute-done.refs_0_), channel_id=1, source_target_pairs={{0,4},{4,8},{8,12},{12,14},{14,10},{10,6},{6,2},{2,0},{5,1},{9,5},... | collective-permute-start | bytes 1327112 | tf_op jit(solution)/shard_map/ppermute | solution.py:248
  13.7 9.5 %collective-permute-start.7 = (bf16[576,384]{1,0:T(8,128)(2,1)S(1)}, bf16[576,384]{1,0:T(8,128)(2,1)S(1)}, u32[]{:S(2)}, u32[]{:S(2)}) collective-permute-start(bf16[576,384]{1,0:T(8,128)(2,1)S(1)} %collective-permute-done.6.refs_0_), channel_id=1, source_target_pairs={{0,4},{4,8},{8,12},{12,14},{14,10},{10,6},{6,2},{2,0},{5,1},{9,5},... | collective-permute-start | bytes 1327112 | tf_op jit(solution)/shard_map/ppermute | solution.py:248
  18.5 9.5 %collective-permute-start.2 = (bf16[576,384]{1,0:T(8,128)(2,1)S(1)}, bf16[576,384]{1,0:T(8,128)(2,1)S(1)}, u32[]{:S(2)}, u32[]{:S(2)}) collective-permute-start(bf16[576,384]{1,0:T(8,128)(2,1)S(1)} %collective-permute-done.1.refs_0_), channel_id=1, source_target_pairs={{0,4},{4,8},{8,12},{12,14},{14,10},{10,6},{6,2},{2,0},{5,1},{9,5},... | collective-permute-start | bytes 1327112 | tf_op jit(solution)/shard_map/ppermute | solution.py:248
  20.6 10.3 %collective-permute-start.14 = (bf16[576,384]{1,0:T(8,128)(2,1)S(1)}, bf16[576,384]{1,0:T(8,128)(2,1)S(1)}, u32[]{:S(2)}, u32[]{:S(2)}) collective-permute-start(bf16[576,384]{1,0:T(8,128)(2,1)S(1)} %collective-permute-done.refs_0_), channel_id=1, source_target_pairs={{0,1},{1,0},{2,3},{3,2},{4,5},{5,4},{6,7},{7,6},{8,9},{9,8},{10,11... | collective-permute-start | bytes 1327112 | tf_op jit(solution)/shard_map/ppermute | solution.py:250
  21.9 9.2 %collective-permute-start.13 = (bf16[576,384]{1,0:T(8,128)(2,1)S(1)}, bf16[576,384]{1,0:T(8,128)(2,1)S(1)}, u32[]{:S(2)}, u32[]{:S(2)}) collective-permute-start(bf16[576,384]{1,0:T(8,128)(2,1)S(1)} %collective-permute-done.6.refs_0_), channel_id=1, source_target_pairs={{0,1},{1,0},{2,3},{3,2},{4,5},{5,4},{6,7},{7,6},{8,9},{9,8},{10,11... | collective-permute-start | bytes 1327112 | tf_op jit(solution)/shard_map/ppermute | solution.py:250
  23.2 23.9 %collective-permute-start.8 = (bf16[576,384]{1,0:T(8,128)(2,1)S(1)}, bf16[576,384]{1,0:T(8,128)(2,1)S(1)}, u32[]{:S(2)}, u32[]{:S(2)}) collective-permute-start(bf16[576,384]{1,0:T(8,128)(2,1)S(1)} %collective-permute-done.7.refs_0_), channel_id=1, source_target_pairs={{0,4},{4,8},{8,12},{12,14},{14,10},{10,6},{6,2},{2,0},{5,1},{9,5},... | collective-permute-start | bytes 1327112 | tf_op jit(solution)/shard_map/ppermute | solution.py:248
  28.0 23.0 %collective-permute-start.3 = (bf16[576,384]{1,0:T(8,128)(2,1)S(1)}, bf16[576,384]{1,0:T(8,128)(2,1)S(1)}, u32[]{:S(2)}, u32[]{:S(2)}) collective-permute-start(bf16[576,384]{1,0:T(8,128)(2,1)S(1)} %collective-permute-done.2.refs_0_), channel_id=1, source_target_pairs={{0,4},{4,8},{8,12},{12,14},{14,10},{10,6},{6,2},{2,0},{5,1},{9,5},... | collective-permute-start | bytes 1327112 | tf_op jit(solution)/shard_map/ppermute | solution.py:248
  29.6 29.4 %collective-permute-start.12 = (bf16[576,384]{1,0:T(8,128)(2,1)S(1)}, bf16[576,384]{1,0:T(8,128)(2,1)S(1)}, u32[]{:S(2)}, u32[]{:S(2)}) collective-permute-start(bf16[576,384]{1,0:T(8,128)(2,1)S(1)} %collective-permute-done.1.refs_0_), channel_id=1, source_target_pairs={{0,1},{1,0},{2,3},{3,2},{4,5},{5,4},{6,7},{7,6},{8,9},{9,8},{10,11... | collective-permute-start | bytes 1327112 | tf_op jit(solution)/shard_map/ppermute | solution.py:250
  31.0 31.9 %collective-permute-start.11 = (bf16[576,384]{1,0:T(8,128)(2,1)S(1)}, bf16[576,384]{1,0:T(8,128)(2,1)S(1)}, u32[]{:S(2)}, u32[]{:S(2)}) collective-permute-start(bf16[576,384]{1,0:T(8,128)(2,1)S(1)} %collective-permute-done.7.refs_0_), channel_id=1, source_target_pairs={{0,1},{1,0},{2,3},{3,2},{4,5},{5,4},{6,7},{7,6},{8,9},{9,8},{10,11... | collective-permute-start | bytes 1327112 | tf_op jit(solution)/shard_map/ppermute | solution.py:250
  31.1 35.4 %collective-permute-start.10 = (bf16[576,384]{1,0:T(8,128)(2,1)S(1)}, bf16[576,384]{1,0:T(8,128)(2,1)S(1)}, u32[]{:S(2)}, u32[]{:S(2)}) collective-permute-start(bf16[576,384]{1,0:T(8,128)(2,1)S(1)} %collective-permute-done.2.refs_0_), channel_id=1, source_target_pairs={{0,1},{1,0},{2,3},{3,2},{4,5},{5,4},{6,7},{7,6},{8,9},{9,8},{10,11... | collective-permute-start | bytes 1327112 | tf_op jit(solution)/shard_map/ppermute | solution.py:250
  31.7 3.2 %copy-start.1 = (bf16[96,64,576]{2,1,0:T(8,128)(2,1)S(1)}, bf16[96,64,576]{2,1,0:T(8,128)(2,1)}, u32[]{:S(2)}) copy-start(bf16[96,64,576]{2,1,0:T(8,128)(2,1)} %query.1) | copy-start | bytes 21233668
  35.0 12.3 %copy-start.2 = (bf16[1,384,576]{1,2,0:T(8,128)(2,1)S(1)}, bf16[1,384,576]{1,2,0:T(8,128)(2,1)}, u32[]{:S(2)}) copy-start(bf16[1,384,576]{1,2,0:T(8,128)(2,1)} %param.9) | copy-start | bytes 1327108
  47.1 24.0 %collective-permute-start.9 = (bf16[576,384]{1,0:T(8,128)(2,1)S(1)}, bf16[576,384]{1,0:T(8,128)(2,1)S(1)}, u32[]{:S(2)}, u32[]{:S(2)}) collective-permute-start(bf16[576,384]{1,0:T(8,128)(2,1)S(1)} %collective-permute-done.8.refs_0_), channel_id=1, source_target_pairs={{0,1},{1,0},{2,3},{3,2},{4,5},{5,4},{6,7},{7,6},{8,9},{9,8},{10,11... | collective-permute-start | bytes 1327112 | tf_op jit(solution)/shard_map/ppermute | solution.py:250
  51.0 23.9 %collective-permute-start.4 = (bf16[576,384]{1,0:T(8,128)(2,1)S(1)}, bf16[576,384]{1,0:T(8,128)(2,1)S(1)}, u32[]{:S(2)}, u32[]{:S(2)}) collective-permute-start(bf16[576,384]{1,0:T(8,128)(2,1)S(1)} %collective-permute-done.3.refs_0_), channel_id=1, source_target_pairs={{0,1},{1,0},{2,3},{3,2},{4,5},{5,4},{6,7},{7,6},{8,9},{9,8},{10,11... | collective-permute-start | bytes 1327112 | tf_op jit(solution)/shard_map/ppermute | solution.py:250
